TPU v7x, 512 devices: a whole 4x8x8 slice. The times are simulated.
512 devices in a mesh: sec: 8 (over y), rad: 16 (over z, x_hi), ax: 4 (over x_lo, core).
Axes of the slice: x: 4 (x_hi: 2, x_lo: 2; x = x_hi * 2 + x_lo), y: 8, z: 8, core: 2. Of those that a mesh axis runs over, the one named last changes fastest.
Arguments:
- state: float32 [5, 8, 1024, 2048], P(None, 'ax', 'rad', 'sec'), may hold values from -1.6 to 4, as said below
- coarsen: int32 [16], replicated, may hold values from 1 to 16, as said below
Outputs:
- tendency: float32 [5, 8, 1024, 2048], P(None, 'ax', 'rad', 'sec')
Inputs may be any that keep to these rules, and one draw needn't show every extreme that they name: `coarsen`: each entry is a power of two; cycle 0 takes 16 and cycle 16 - 1 takes 1. state[0] (density) lies in 0.6 to 1.4, the momenta in -1.6 to 1.6, state[4] (energy) in 2.5 to 4.0.
All inputs are finite; a program needn't handle non-finite values.
Results may differ from a plain program's by a relative error of at most 0.0003.
Values sent between devices are 32-bit elements; how exact they have to be, the bound alone decides.
A program may use at most 64 MiB of HBM per device.

v0:
```python
import math
import jax
import jax.numpy as jnp
from jax import lax
from jax.sharding import PartitionSpec as P

R_NEAR = 16
GAMMA = 1.4
KAPPA = 1.44


def padded_2(value, sides, width):
    for axis, dim in sides:
        size, length = (lax.axis_size(axis), value.shape[dim])
        up = [(i, (i + 1) % size) for i in range(size)]
        down = [(j, i) for i, j in up]
        last = lax.slice_in_dim(value, length - width, length, axis=dim)
        first = lax.slice_in_dim(value, 0, width, axis=dim)
        before = lax.ppermute(last, axis, up)
        after = lax.ppermute(first, axis, down)
        value = jnp.concatenate([before, value, after], axis=dim)
    return value


def spread(value, axis, root):
    mine = lax.axis_index(axis) == root
    return lax.psum(jnp.where(mine, value, jnp.zeros_like(value)), axis)


def body(state, coarsen):
    fields, planes, cycles_dev, cells_dev = state.shape
    sec_count = lax.axis_size("sec")
    rad_count = lax.axis_size("rad")
    ax_count = lax.axis_size("ax")
    sec_index = lax.axis_index("sec")
    rad_index = lax.axis_index("rad")
    ax_index = lax.axis_index("ax")
    total_cells = cells_dev * sec_count
    dtheta = 2.0 * math.pi / total_cells
    padded = padded_2(state, (("sec", 3), ("rad", 2), ("ax", 1)), 1)
    plane_pos = ax_index * planes + jnp.arange(-1, planes + 1, dtype=jnp.int32)
    cycle_pos = rad_index * cycles_dev + jnp.arange(-1, cycles_dev + 1, dtype=jnp.int32)
    inside_ax = ((plane_pos >= 0) & (plane_pos < planes * ax_count)).astype(jnp.float32)
    inside_rad = ((cycle_pos >= 0) & (cycle_pos < cycles_dev * rad_count)).astype(jnp.float32)
    ghost_plane = jnp.arange(planes + 2) % (planes + 1) == 0
    ghost_cycle = jnp.arange(cycles_dev + 2) % (cycles_dev + 1) == 0
    ghost_cell = jnp.arange(cells_dev + 2) % (cells_dev + 1) == 0
    ghosts = (
        ghost_plane.astype(jnp.int32)[:, None, None]
        + ghost_cycle.astype(jnp.int32)[None, :, None]
        + ghost_cell.astype(jnp.int32)[None, None, :]
    )
    corner = ghosts >= 2
    density = jnp.where(corner, 1.0, padded[0])
    mom_ax = padded[1]
    mom_rad = padded[2]
    mom_az = padded[3]
    energy = padded[4]
    vel_ax = mom_ax / density
    vel_rad = mom_rad / density
    vel_az = mom_az / density
    pressure = (GAMMA - 1.0) * (
        energy - 0.5 * (mom_ax * vel_ax + mom_rad * vel_rad + mom_az * vel_az)
    )
    radius_pad = cycle_pos.astype(jnp.float32) + 0.5
    flux_ax = jnp.stack(
        [
            mom_ax,
            mom_ax * vel_ax + pressure,
            mom_rad * vel_ax,
            mom_az * vel_ax,
            (energy + pressure) * vel_ax,
        ]
    )
    flux_ax = flux_ax * inside_ax[None, :, None, None]
    flux_rad = jnp.stack(
        [
            mom_rad,
            mom_ax * vel_rad,
            mom_rad * vel_rad + pressure,
            mom_az * vel_rad,
            (energy + pressure) * vel_rad,
        ]
    )
    flux_rad = flux_rad * (radius_pad * inside_rad)[None, None, :, None]
    flux_az = jnp.stack(
        [
            mom_az,
            mom_ax * vel_az,
            mom_rad * vel_az,
            mom_az * vel_az + pressure,
            (energy + pressure) * vel_az,
        ]
    )
    radius = radius_pad[1:-1][:, None]
    tendency = -(flux_ax[:, 2:, 1:-1, 1:-1] - flux_ax[:, :-2, 1:-1, 1:-1]) * 0.5
    tendency = (
        tendency - (flux_rad[:, 1:-1, 2:, 1:-1] - flux_rad[:, 1:-1, :-2, 1:-1]) * 0.5 / radius
    )
    tendency = tendency - (flux_az[:, 1:-1, 1:-1, 2:] - flux_az[:, 1:-1, 1:-1, :-2]) * 0.5 / (
        radius * dtheta
    )
    inner_press = pressure[1:-1, 1:-1, 1:-1]
    inner_mom_az = mom_az[1:-1, 1:-1, 1:-1]
    inner_mom_rad = mom_rad[1:-1, 1:-1, 1:-1]
    inner_vel_az = vel_az[1:-1, 1:-1, 1:-1]
    zero_part = jnp.zeros_like(inner_press)
    source = jnp.stack(
        [
            zero_part,
            zero_part,
            (inner_press + inner_mom_az * inner_vel_az) / radius,
            -(inner_mom_rad * inner_vel_az) / radius,
            zero_part,
        ]
    )
    tendency = tendency + source
    own_pos = sec_index * cells_dev + jnp.arange(cells_dev, dtype=jnp.int32)

    def kernel(cycle_factor, cycle_blocks, log_ratio, scale_const, columns):
        rows_coarse = own_pos // cycle_factor
        columns_coarse = columns // cycle_factor
        distance = ((rows_coarse[:, None] - columns_coarse[None, :]) % cycle_blocks).astype(
            jnp.float32
        )
        blocks_f = cycle_blocks.astype(jnp.float32)
        return (jnp.exp(distance * log_ratio) + jnp.exp((blocks_f - distance) * log_ratio)) / (
            scale_const * cycle_factor.astype(jnp.float32)
        )

    near_axis = tendency[:, :, :R_NEAR, :]
    cycle_lines = jnp.transpose(near_axis, (2, 0, 1, 3)).reshape(R_NEAR, fields * planes, cells_dev)
    shared = spread(cycle_lines, "rad", 0)
    per_device = R_NEAR // rad_count
    my_cycles = lax.dynamic_slice_in_dim(shared, rad_index * per_device, per_device, 0)
    selector = (rad_index * per_device + jnp.arange(per_device, dtype=jnp.int32))[
        :, None
    ] == jnp.arange(coarsen.shape[0], dtype=jnp.int32)[None, :]
    factor = jnp.sum(jnp.where(selector, coarsen[None, :], 0), axis=1)
    blocks = total_cells // factor
    factor_f = factor.astype(jnp.float32)
    stiffness = KAPPA / (factor_f * dtheta) ** 2
    inverse_half = 0.5 / stiffness
    one_minus = jnp.sqrt(inverse_half * (2.0 + inverse_half)) - inverse_half
    log_ratio = jnp.log1p(-one_minus)
    scale_const = (
        stiffness
        * one_minus
        * (2.0 - one_minus)
        / (1.0 - one_minus)
        * -jnp.expm1(blocks.astype(jnp.float32) * log_ratio)
    )
    portion = lax.all_gather(my_cycles, "sec", axis=2, tiled=True)
    columns = jnp.arange(portion.shape[2], dtype=jnp.int32)

    def per_cycle(cycle_item):
        lines_one, cycle_factor, cycle_blocks, cycle_log, cycle_scale = cycle_item
        table = kernel(cycle_factor, cycle_blocks, cycle_log, cycle_scale, columns)
        return jnp.einsum("lq,pq->lp", lines_one, table, precision=lax.Precision.HIGHEST)

    smoothed = lax.map(per_cycle, (portion, factor, blocks, log_ratio, scale_const))
    result = lax.all_gather(smoothed, "rad", axis=0, tiled=True)
    restored = jnp.transpose(result.reshape(R_NEAR, fields, planes, cells_dev), (1, 2, 0, 3))
    near_new = jnp.where(rad_index == 0, restored, near_axis)
    return jnp.concatenate([near_new, tendency[:, :, R_NEAR:, :]], axis=2)


def solution(mesh):
    return jax.shard_map(
        body,
        mesh=mesh,
        in_specs=(P(None, "ax", "rad", "sec"), P()),
        out_specs=P(None, "ax", "rad", "sec"),
        check_vma=False,
    )
```

profile of v0, /device:TPU:6, one launch (start us, length us, event | category | flops | bytes accessed | tf_op | source)
XLA Modules:
  0.0 309.1 jit_solution(6789559779002969412)
XLA Ops:
  6.5 0.0 all-reduce.2.cloned.1.call-start
  6.5 1.3 fusion.47
  7.8 3.5 %collective-permute-start = (f32[5,2,64,1]{3,2,1,0:T(8,128)S(1)}, f32[5,2,64,1]{3,2,1,0:T(8,128)S(1)}, u32[]{:S(2)}, u32[]{:S(2)}) collective-permute-start(f32[5,2,64,1]{3,2,1,0:T(8,128)S(1)} %get-tuple-element.59), channel_id=1, source_target_pairs={{0,64},{64,128},{128,192},{192,256},{256,320},{320,384},{384,448},... | collective-permute-start | bytes 7688 | tf_op jit(solution)/shard_map/ppermute | solution.py:19
  11.3 3.8 %collective-permute-start.1 = (f32[5,2,64,1]{3,2,1,0:T(8,128)S(1)}, f32[5,2,64,1]{3,2,1,0:T(8,128)S(1)}, u32[]{:S(2)}, u32[]{:S(2)}) collective-permute-start(f32[5,2,64,1]{3,2,1,0:T(8,128)S(1)} %get-tuple-element.60), channel_id=1, source_target_pairs={{64,0},{128,64},{192,128},{256,192},{320,256},{384,320},{448,384},... | collective-permute-start | bytes 7688 | tf_op jit(solution)/shard_map/ppermute | solution.py:20
  15.2 0.1 broadcast_multiply_fusion.2
  15.2 1.4 fusion.44
  16.6 4.3 %collective-permute-done = f32[5,2,64,1]{3,2,1,0:T(8,128)S(1)} collective-permute-done((f32[5,2,64,1]{3,2,1,0:T(8,128)S(1)}, f32[5,2,64,1]{3,2,1,0:T(8,128)S(1)}, u32[]{:S(2)}, u32[]{:S(2)}) %collective-permute-start) | collective-permute-done | bytes 2592 | tf_op jit(solution)/shard_map/ppermute | solution.py:19
  20.9 1.5 collective-permute-done.1
  22.4 1.1 pad_maximum_fusion.5
  23.5 5.1 %collective-permute-start.2 = (f32[5,2,1,258]{3,2,1,0:T(1,128)S(1)}, f32[5,2,1,258]{3,2,1,0:T(1,128)S(1)}, u32[]{:S(2)}, u32[]{:S(2)}) collective-permute-start(f32[5,2,1,258]{3,2,1,0:T(1,128)S(1)} %get-tuple-element.53), channel_id=1, source_target_pairs={{0,4},{4,8},{8,12},{12,16},{16,20},{20,24},{24,28},{28,32},{32,36}... | collective-permute-start | bytes 30968 | tf_op jit(solution)/shard_map/ppermute | solution.py:19
  28.6 2.2 collective-permute-start.3
  30.9 0.0 collective-permute-done.2
  30.9 5.8 %collective-permute-done.3 = f32[5,2,1,258]{3,2,1,0:T(1,128)S(1)} collective-permute-done((f32[5,2,1,258]{3,2,1,0:T(1,128)S(1)}, f32[5,2,1,258]{3,2,1,0:T(1,128)S(1)}, u32[]{:S(2)}, u32[]{:S(2)}) %collective-permute-start.3) | collective-permute-done | bytes 10352 | tf_op jit(solution)/shard_map/ppermute | solution.py:20
  36.6 0.5 pad_maximum_fusion.1
  37.1 0.1 fusion.46
  37.2 0.5 copy.5
  37.7 1.9 collective-permute-start.4
  39.6 0.5 copy.6
  40.2 3.6 %collective-permute-start.5 = (f32[5,1,66,258]{3,1,2,0:T(1,128)S(1)}, f32[5,1,66,258]{3,1,2,0:T(1,128)S(1)}, u32[]{:S(2)}, u32[]{:S(2)}) collective-permute-start(f32[5,1,66,258]{3,1,2,0:T(1,128)S(1)} %copy.6), channel_id=1, source_target_pairs={{1,0},{2,1},{3,2},{0,3},{5,4},{6,5},{7,6},{4,7},{9,8},{10,9},{11,1... | collective-permute-start | bytes 1021688 | tf_op jit(solution)/shard_map/ppermute | solution.py:20
  43.9 0.1 pad.5.clone
  44.7 0.1 broadcast_add_fusion
  44.7 6.0 %collective-permute-done.4 = f32[5,1,66,258]{3,1,2,0:T(1,128)S(1)} collective-permute-done((f32[5,1,66,258]{3,1,2,0:T(1,128)S(1)}, f32[5,1,66,258]{3,1,2,0:T(1,128)S(1)}, u32[]{:S(2)}, u32[]{:S(2)}) %collective-permute-start.4) | collective-permute-done | bytes 340592 | tf_op jit(solution)/shard_map/ppermute | solution.py:19
  50.8 0.1 collective-permute-done.5
  51.0 0.5 pad_maximum_fusion
  51.5 0.2 slice_bitcast_fusion.3
  51.7 0.2 fusion.28
  51.9 0.3 add_dynamic-update-slice_fusion.2
  52.2 0.1 multiply_dynamic-update-slice_fusion.8
  52.2 0.1 multiply_dynamic-update-slice_fusion.7
  52.4 0.1 multiply_dynamic-update-slice_fusion.1
  52.4 0.1 add_dynamic-update-slice_fusion
  52.5 0.2 multiply_dynamic-update-slice_fusion.6
  52.7 0.1 multiply_dynamic-update-slice_fusion.4
  52.8 0.1 multiply_dynamic-update-slice_fusion.3
  52.9 0.4 broadcast_multiply_fusion
  53.3 0.3 fusion.32
  53.6 1.1 fusion.19
  54.7 0.7 slice_select_fusion.1
  55.4 0.0 all-reduce.2.cloned.1.call-update
  55.4 0.8 and_select_fusion
  58.5 0.8 add_select_fusion.1
  59.4 161.4 %all-reduce.2.cloned.1.call-done = f32[16,10,256]{2,0,1:T(8,128)} async-done(((f32[16,10,256]{2,0,1:T(8,128)}), f32[16,10,256]{2,0,1:T(8,128)}) %all-reduce.2.cloned.1.call-update) | async-done | bytes 163856 | tf_op jit(solution)/shard_map/psum | solution.py:27
  220.8 0.9 constant_dynamic-slice_fusion
  221.7 16.7 %all_gather.6 = f32[1,10,2048]{2,0,1:T(1,128)S(1)} all-gather(f32[1,10,256]{2,0,1:T(1,128)S(1)} %constant_dynamic-slice_fusion), channel_id=1, replica_groups=mesh['sec'=8,'rad'=16,'ax'=4] {'sec'}, dimensions={2}, use_global_device_ids=true | all-gather | bytes 92160 | tf_op jit(solution)/shard_map/all_gather | solution.py:153
  238.4 22.6 %fusion.7 = f32[1,10,256]{2,1,0:T(8,128)S(1)} fusion(f32[]{:T(128)S(6)} %mul.233, f32[]{:T(128)S(6)} %convert_element_type.66, f32[]{:T(128)} %bitcast.13, s32[]{:T(128)S(6)} %select_n.132, s32[2048]{0:T(1024)S(1)} %add_select_fusion.1, s32[256]{0:T(256)S(1)} %and_select_fusion, pred[]{:T(512)S(6)} %lt.63, f32[1,10,2048]{2,0,1:T(1,128)S(1)} %all_gather.6), kind=kOutput, calls=%fused_computation.10 | convolution fusion | flops 70254592 | bytes 101393 | tf_op jit(solution)/shard_map/while/body/eval_jaxpr/lq,pq->lp/dot_general | solution.py:159
  261.0 40.3 %all-gather.1 = f32[16,10,256]{2,1,0:T(8,128)S(1)} all-gather(f32[1,10,256]{2,1,0:T(8,128)S(1)} %fusion.7), channel_id=2, replica_groups=mesh['sec'=8,'rad'=16,'ax'=4] {'rad'}, dimensions={0}, use_global_device_ids=true | all-gather | bytes 174080 | tf_op jit(solution)/shard_map/all_gather | solution.py:162
  301.2 0.1 copy.9
  301.4 0.9 pad_maximum_fusion.2
  (14 shorter events, 0.2 us)
Async XLA Ops:
  6.5 30.1 %copy-start = (f32[5,2,64,256]{3,2,1,0:T(8,128)S(1)}, f32[5,2,64,256]{3,2,1,0:T(8,128)}, u32[]{:S(2)}) copy-start(f32[5,2,64,256]{3,2,1,0:T(8,128)} %param.2) | copy-start | bytes 1966084
  6.5 214.2 %all-reduce.2.cloned.1.call-start = ((), (), s32[]{:S(2)}) async-start(), calls=%async_computation | async-start | bytes 327680 | tf_op jit(solution)/shard_map/psum | solution.py:27
  7.8 13.1 %collective-permute-start = (f32[5,2,64,1]{3,2,1,0:T(8,128)S(1)}, f32[5,2,64,1]{3,2,1,0:T(8,128)S(1)}, u32[]{:S(2)}, u32[]{:S(2)}) collective-permute-start(f32[5,2,64,1]{3,2,1,0:T(8,128)S(1)} %get-tuple-element.59), channel_id=1, source_target_pairs={{0,64},{64,128},{128,192},{192,256},{256,320},{320,384},{384,448},... | collective-permute-start | bytes 7688 | tf_op jit(solution)/shard_map/ppermute | solution.py:19
  11.3 11.1 %collective-permute-start.1 = (f32[5,2,64,1]{3,2,1,0:T(8,128)S(1)}, f32[5,2,64,1]{3,2,1,0:T(8,128)S(1)}, u32[]{:S(2)}, u32[]{:S(2)}) collective-permute-start(f32[5,2,64,1]{3,2,1,0:T(8,128)S(1)} %get-tuple-element.60), channel_id=1, source_target_pairs={{64,0},{128,64},{192,128},{256,192},{320,256},{384,320},{448,384},... | collective-permute-start | bytes 7688 | tf_op jit(solution)/shard_map/ppermute | solution.py:20
  23.5 7.4 %collective-permute-start.2 = (f32[5,2,1,258]{3,2,1,0:T(1,128)S(1)}, f32[5,2,1,258]{3,2,1,0:T(1,128)S(1)}, u32[]{:S(2)}, u32[]{:S(2)}) collective-permute-start(f32[5,2,1,258]{3,2,1,0:T(1,128)S(1)} %get-tuple-element.53), channel_id=1, source_target_pairs={{0,4},{4,8},{8,12},{12,16},{16,20},{20,24},{24,28},{28,32},{32,36}... | collective-permute-start | bytes 30968 | tf_op jit(solution)/shard_map/ppermute | solution.py:19
  28.6 8.0 %collective-permute-start.3 = (f32[5,2,1,258]{3,2,1,0:T(1,128)S(1)}, f32[5,2,1,258]{3,2,1,0:T(1,128)S(1)}, u32[]{:S(2)}, u32[]{:S(2)}) collective-permute-start(f32[5,2,1,258]{3,2,1,0:T(1,128)S(1)} %get-tuple-element.54), channel_id=1, source_target_pairs={{4,0},{8,4},{12,8},{16,12},{20,16},{24,20},{28,24},{32,28},{36,32}... | collective-permute-start | bytes 30968 | tf_op jit(solution)/shard_map/ppermute | solution.py:20
  37.7 13.0 %collective-permute-start.4 = (f32[5,1,66,258]{3,1,2,0:T(1,128)S(1)}, f32[5,1,66,258]{3,1,2,0:T(1,128)S(1)}, u32[]{:S(2)}, u32[]{:S(2)}) collective-permute-start(f32[5,1,66,258]{3,1,2,0:T(1,128)S(1)} %copy.5), channel_id=1, source_target_pairs={{0,1},{1,2},{2,3},{3,0},{4,5},{5,6},{6,7},{7,4},{8,9},{9,10},{10,1... | collective-permute-start | bytes 1021688 | tf_op jit(solution)/shard_map/ppermute | solution.py:19
  40.2 10.7 %collective-permute-start.5 = (f32[5,1,66,258]{3,1,2,0:T(1,128)S(1)}, f32[5,1,66,258]{3,1,2,0:T(1,128)S(1)}, u32[]{:S(2)}, u32[]{:S(2)}) collective-permute-start(f32[5,1,66,258]{3,1,2,0:T(1,128)S(1)} %copy.6), channel_id=1, source_target_pairs={{1,0},{2,1},{3,2},{0,3},{5,4},{6,5},{7,6},{4,7},{9,8},{10,9},{11,1... | collective-permute-start | bytes 1021688 | tf_op jit(solution)/shard_map/ppermute | solution.py:20
Sparse Core Ops, SparseCore 0:
  55.5 165.2 all-reduce.1
where the time goes:
time: 310 us; the launch traced here: 309 us
  waiting for transfers between devices  179 us (58%)
  blocking collectives  57 us (18%)
  matrix products  22.6 us (7%)
  starting transfers between devices  20.2 us (7%)
  between operations  16.7 us (5%)
  other arithmetic  9.79 us (3%)
  local copies, waits for them, and re-layouts  3.82 us (1%)
    psum x1, waiting for transfers between devices, spread(): return lax.psum(jnp.where(mine, value, jnp.zeros_like(value)), axis)  161 us
    all_gather x1, blocking collectives, body(): result = lax.all_gather(smoothed, 'rad', axis=0, tiled=True)  40.3 us
    dot_general x1, matrix products, per_cycle(): jnp.einsum('lq,pq->lp', lines_one, table, precision=lax.Precision.HIGHEST)  22.6 us
    all_gather x1, blocking collectives, body(): portion = lax.all_gather(my_cycles, 'sec', axis=2, tiled=True)  16.7 us
    ppermute x3, starting transfers between devices, padded_2(): before = lax.ppermute(last, axis, up)  10.5 us
    ppermute x3, waiting for transfers between devices, padded_2(): before = lax.ppermute(last, axis, up)  10.3 us
    ppermute x3, starting transfers between devices, padded_2(): after = lax.ppermute(first, axis, down)  9.68 us
    ppermute x3, waiting for transfers between devices, padded_2(): after = lax.ppermute(first, axis, down)  7.38 us
  transfers between devices with their start and end apart: 7, of which 6 were waited for; matrix products, arithmetic and copies ran while one was open for 1% of the time, Pallas kernels for 0%

commit v1 on v0

--- a/solution.py
+++ b/solution.py
@@ -7,6 +7,24 @@
 R_NEAR = 16
 GAMMA = 1.4
 KAPPA = 1.44
+
+
+def laid_out(blocks, dim):
+    blocks = jnp.moveaxis(blocks, 0, dim)
+    lengths = blocks.shape
+    return blocks.reshape(*lengths[:dim], lengths[dim] * lengths[dim + 1], *lengths[dim + 2 :])
+
+
+def doubled(value, axis):
+    size = lax.axis_size(axis)
+    tiles = value[None]
+    for level in range(size.bit_length() - 1):
+        bit = 1 << level
+        partner_block = lax.ppermute(tiles, axis, [(i, i ^ bit) for i in range(size)])
+        both = jnp.stack([tiles, partner_block])
+        upper = lax.axis_index(axis) >> level & 1
+        tiles = jnp.where(upper == 0, both, both[::-1]).reshape(-1, *value.shape)
+    return tiles
 
 
 def padded_2(value, sides, width):
@@ -150,7 +168,7 @@
         / (1.0 - one_minus)
         * -jnp.expm1(blocks.astype(jnp.float32) * log_ratio)
     )
-    portion = lax.all_gather(my_cycles, "sec", axis=2, tiled=True)
+    portion = laid_out(doubled(my_cycles, "sec"), 2)
     columns = jnp.arange(portion.shape[2], dtype=jnp.int32)
 
     def per_cycle(cycle_item):

time: 310 us -> 317 us (1.023)
  blocking collectives: 57 us -> 40.3 us
  starting transfers between devices: 20.2 us -> 35.5 us
  waiting for transfers between devices: 179 us -> 187 us
    all_gather x1 -> x0, blocking collectives: 16.7 us -> none  [body(): portion = lax.all_gather(my_cycles, 'sec', axis=2, tiled=True)]
    ppermute x0 -> x3, starting transfers between devices: none -> 15.3 us  [doubled(): lax.ppermute(tiles, axis, [(i, i ^ bit) for i in range(size)])]
    psum x1, waiting for transfers between devices: 161 us -> 165 us  [spread(): return lax.psum(jnp.where(mine, value, jnp.zeros_like(value)), axis)]
  transfers between devices with their start and end apart: 7 -> 10, of which waited for: 6 -> 8; matrix products, arithmetic and copies ran while one was open for 1% -> 1% of each run, Pallas kernels for 0% -> 0%
where the time goes in v1:
time: 317 us; the launch traced here: 316 us
  waiting for transfers between devices  187 us (59%)
  blocking collectives  40.3 us (13%)
  starting transfers between devices  35.5 us (11%)
  matrix products  22.6 us (7%)
  between operations  16.6 us (5%)
  other arithmetic  9.25 us (3%)
  local copies, waits for them, and re-layouts  4.43 us (1%)
    psum x1, waiting for transfers between devices, spread(): return lax.psum(jnp.where(mine, value, jnp.zeros_like(value)), axis)  165 us
    all_gather x1, blocking collectives, body(): result = lax.all_gather(smoothed, 'rad', axis=0, tiled=True)  40.3 us
    dot_general x1, matrix products, per_cycle(): jnp.einsum('lq,pq->lp', lines_one, table, precision=lax.Precision.HIGHEST)  22.6 us
    ppermute x3, starting transfers between devices, doubled(): lax.ppermute(tiles, axis, [(i, i ^ bit) for i in range(size)])  15.3 us
    ppermute x3, waiting for transfers between devices, padded_2(): before = lax.ppermute(last, axis, up)  12.4 us
    ppermute x3, starting transfers between devices, padded_2(): before = lax.ppermute(last, axis, up)  10.5 us
    ppermute x3, starting transfers between devices, padded_2(): after = lax.ppermute(first, axis, down)  9.68 us
    ppermute x3, waiting for transfers between devices, padded_2(): after = lax.ppermute(first, axis, down)  7.38 us
  transfers between devices with their start and end apart: 10, of which 8 were waited for; matrix products, arithmetic and copies ran while one was open for 1% of the time, Pallas kernels for 0%

profile of v1, /device:TPU:6, one launch (start us, length us, event | category | flops | bytes accessed | tf_op | source)
XLA Modules:
  0.0 316.2 jit_solution(1509740572476462167)
XLA Ops:
  6.5 1.3 fusion.47
  7.8 3.5 %collective-permute-start = (f32[5,2,64,1]{3,2,1,0:T(8,128)S(1)}, f32[5,2,64,1]{3,2,1,0:T(8,128)S(1)}, u32[]{:S(2)}, u32[]{:S(2)}) collective-permute-start(f32[5,2,64,1]{3,2,1,0:T(8,128)S(1)} %get-tuple-element.59), channel_id=1, source_target_pairs={{0,64},{64,128},{128,192},{192,256},{256,320},{320,384},{384,448},... | collective-permute-start | bytes 7688 | tf_op jit(solution)/shard_map/ppermute | solution.py:37
  11.3 3.8 %collective-permute-start.1 = (f32[5,2,64,1]{3,2,1,0:T(8,128)S(1)}, f32[5,2,64,1]{3,2,1,0:T(8,128)S(1)}, u32[]{:S(2)}, u32[]{:S(2)}) collective-permute-start(f32[5,2,64,1]{3,2,1,0:T(8,128)S(1)} %get-tuple-element.60), channel_id=1, source_target_pairs={{64,0},{128,64},{192,128},{256,192},{320,256},{384,320},{448,384},... | collective-permute-start | bytes 7688 | tf_op jit(solution)/shard_map/ppermute | solution.py:38
  15.2 0.1 broadcast_multiply_fusion.2
  15.3 5.6 %collective-permute-done = f32[5,2,64,1]{3,2,1,0:T(8,128)S(1)} collective-permute-done((f32[5,2,64,1]{3,2,1,0:T(8,128)S(1)}, f32[5,2,64,1]{3,2,1,0:T(8,128)S(1)}, u32[]{:S(2)}, u32[]{:S(2)}) %collective-permute-start) | collective-permute-done | bytes 2592 | tf_op jit(solution)/shard_map/ppermute | solution.py:37
  20.9 1.5 collective-permute-done.1
  22.4 1.1 pad_maximum_fusion.8
  23.5 5.1 %collective-permute-start.2 = (f32[5,2,1,258]{3,2,1,0:T(1,128)S(1)}, f32[5,2,1,258]{3,2,1,0:T(1,128)S(1)}, u32[]{:S(2)}, u32[]{:S(2)}) collective-permute-start(f32[5,2,1,258]{3,2,1,0:T(1,128)S(1)} %get-tuple-element.53), channel_id=1, source_target_pairs={{0,4},{4,8},{8,12},{12,16},{16,20},{20,24},{24,28},{28,32},{32,36}... | collective-permute-start | bytes 30968 | tf_op jit(solution)/shard_map/ppermute | solution.py:37
  28.6 2.2 collective-permute-start.3
  30.9 5.8 %collective-permute-done.3 = f32[5,2,1,258]{3,2,1,0:T(1,128)S(1)} collective-permute-done((f32[5,2,1,258]{3,2,1,0:T(1,128)S(1)}, f32[5,2,1,258]{3,2,1,0:T(1,128)S(1)}, u32[]{:S(2)}, u32[]{:S(2)}) %collective-permute-start.3) | collective-permute-done | bytes 10352 | tf_op jit(solution)/shard_map/ppermute | solution.py:38
  36.6 0.5 pad_maximum_fusion.1
  37.2 0.5 copy.8
  37.7 1.9 collective-permute-start.4
  39.6 0.5 copy.9
  40.2 3.6 %collective-permute-start.5 = (f32[5,1,66,258]{3,1,2,0:T(1,128)S(1)}, f32[5,1,66,258]{3,1,2,0:T(1,128)S(1)}, u32[]{:S(2)}, u32[]{:S(2)}) collective-permute-start(f32[5,1,66,258]{3,1,2,0:T(1,128)S(1)} %copy.9), channel_id=1, source_target_pairs={{1,0},{2,1},{3,2},{0,3},{5,4},{6,5},{7,6},{4,7},{9,8},{10,9},{11,1... | collective-permute-start | bytes 1021688 | tf_op jit(solution)/shard_map/ppermute | solution.py:38
  43.9 0.1 pad.11.clone
  44.0 6.7 %collective-permute-done.4 = f32[5,1,66,258]{3,1,2,0:T(1,128)S(1)} collective-permute-done((f32[5,1,66,258]{3,1,2,0:T(1,128)S(1)}, f32[5,1,66,258]{3,1,2,0:T(1,128)S(1)}, u32[]{:S(2)}, u32[]{:S(2)}) %collective-permute-start.4) | collective-permute-done | bytes 340592 | tf_op jit(solution)/shard_map/ppermute | solution.py:37
  50.8 0.1 collective-permute-done.5
  51.0 0.5 pad_maximum_fusion
  51.4 0.2 slice_bitcast_fusion.3
  51.7 0.2 fusion.28
  51.9 0.3 add_dynamic-update-slice_fusion.2
  52.2 0.1 multiply_dynamic-update-slice_fusion.7
  52.4 0.1 add_dynamic-update-slice_fusion
  52.5 0.2 multiply_dynamic-update-slice_fusion.6
  52.8 0.1 multiply_dynamic-update-slice_fusion.3
  52.8 0.4 broadcast_multiply_fusion
  53.3 0.3 fusion.32
  53.6 1.1 fusion.19
  54.7 0.7 slice_select_fusion.1
  55.4 165.4 %all-reduce.2.cloned.1.call-done = f32[16,10,256]{2,0,1:T(8,128)} async-done(((f32[16,10,256]{2,0,1:T(8,128)}), f32[16,10,256]{2,0,1:T(8,128)}) %all-reduce.2.cloned.1.call-update) | async-done | bytes 163856 | tf_op jit(solution)/shard_map/psum | solution.py:45
  220.8 0.9 dynamic-slice_bitcast_fusion.1
  221.7 3.4 %collective-permute-start.6 = (f32[1,1,10,256]{3,1,2,0:T(1,128)S(1)}, f32[1,1,10,256]{3,1,2,0:T(1,128)S(1)}, u32[]{:S(2)}, u32[]{:S(2)}) collective-permute-start(f32[1,1,10,256]{3,1,2,0:T(1,128)S(1)} %get-tuple-element.62), channel_id=1, source_target_pairs={{0,64},{64,0},{128,192},{192,128},{256,320},{320,256},{384,448},{4... | collective-permute-start | bytes 30728 | tf_op jit(solution)/shard_map/ppermute | solution.py:23
  225.1 0.6 fusion.44
  226.4 0.9 collective-permute-done.6
  227.3 4.3 %collective-permute-start.7 = (f32[2,1,10,256]{3,1,2,0:T(1,128)S(1)}, f32[2,1,10,256]{3,1,2,0:T(1,128)S(1)}, u32[]{:S(2)}, u32[]{:S(2)}) collective-permute-start(f32[2,1,10,256]{3,1,2,0:T(1,128)S(1)} %get-tuple-element.64), channel_id=1, source_target_pairs={{0,128},{64,192},{128,0},{192,64},{256,384},{320,448},{384,256},{4... | collective-permute-start | bytes 61448 | tf_op jit(solution)/shard_map/ppermute | solution.py:23
  231.7 0.8 add_select_fusion.1
  232.4 1.5 collective-permute-done.7
  234.0 7.6 %collective-permute-start.8 = (f32[4,1,10,256]{3,1,2,0:T(1,128)S(1)}, f32[4,1,10,256]{3,1,2,0:T(1,128)S(1)}, u32[]{:S(2)}, u32[]{:S(2)}) collective-permute-start(f32[4,1,10,256]{3,1,2,0:T(1,128)S(1)} %bitcast.68), channel_id=1, source_target_pairs={{0,256},{64,320},{128,384},{192,448},{256,0},{320,64},{384,128},{4... | collective-permute-start | bytes 122888 | tf_op jit(solution)/shard_map/ppermute | solution.py:23
  241.6 0.8 and_select_fusion
  244.6 0.1 pad_maximum_fusion.3
  244.7 0.5 rev.11
  245.2 0.1 broadcast_select_fusion.1
  245.3 0.1 copy.12
  245.4 22.6 %fusion.7 = f32[1,10,256]{2,1,0:T(8,128)S(1)} fusion(f32[10,2048]{1,0:T(8,128)S(1)} %bitcast.75, f32[]{:T(128)S(6)} %mul.233, f32[]{:T(128)S(6)} %convert_element_type.66, f32[]{:T(128)} %bitcast.24, s32[]{:T(128)S(6)} %select_n.162, s32[2048]{0:T(1024)S(1)} %add_select_fusion.1, s32[256]{0:T(256)S(1)} %and_select_fusion, pred[]{:T(512)S(6)} %lt.63), kind=kOutput, calls=%fused_computation.10 | convolution fusion | flops 70254592 | bytes 101393 | tf_op jit(solution)/shard_map/while/body/eval_jaxpr/lq,pq->lp/dot_general | solution.py:177
  268.0 40.3 %all-gather.1 = f32[16,10,256]{2,1,0:T(8,128)S(1)} all-gather(f32[1,10,256]{2,1,0:T(8,128)S(1)} %fusion.7), channel_id=2, replica_groups=mesh['sec'=8,'rad'=16,'ax'=4] {'rad'}, dimensions={0}, use_global_device_ids=true | all-gather | bytes 174080 | tf_op jit(solution)/shard_map/all_gather | solution.py:180
  308.3 0.1 copy.14
  308.4 0.9 pad_maximum_fusion.2
  (32 shorter events, 0.7 us)
Async XLA Ops:
  6.5 30.1 %copy-start = (f32[5,2,64,256]{3,2,1,0:T(8,128)S(1)}, f32[5,2,64,256]{3,2,1,0:T(8,128)}, u32[]{:S(2)}) copy-start(f32[5,2,64,256]{3,2,1,0:T(8,128)} %param.2) | copy-start | bytes 1966084
  6.5 214.3 %all-reduce.2.cloned.1.call-start = ((), (), s32[]{:S(2)}) async-start(), calls=%async_computation | async-start | bytes 327680 | tf_op jit(solution)/shard_map/psum | solution.py:45
  7.8 13.1 %collective-permute-start = (f32[5,2,64,1]{3,2,1,0:T(8,128)S(1)}, f32[5,2,64,1]{3,2,1,0:T(8,128)S(1)}, u32[]{:S(2)}, u32[]{:S(2)}) collective-permute-start(f32[5,2,64,1]{3,2,1,0:T(8,128)S(1)} %get-tuple-element.59), channel_id=1, source_target_pairs={{0,64},{64,128},{128,192},{192,256},{256,320},{320,384},{384,448},... | collective-permute-start | bytes 7688 | tf_op jit(solution)/shard_map/ppermute | solution.py:37
  11.3 11.1 %collective-permute-start.1 = (f32[5,2,64,1]{3,2,1,0:T(8,128)S(1)}, f32[5,2,64,1]{3,2,1,0:T(8,128)S(1)}, u32[]{:S(2)}, u32[]{:S(2)}) collective-permute-start(f32[5,2,64,1]{3,2,1,0:T(8,128)S(1)} %get-tuple-element.60), channel_id=1, source_target_pairs={{64,0},{128,64},{192,128},{256,192},{320,256},{384,320},{448,384},... | collective-permute-start | bytes 7688 | tf_op jit(solution)/shard_map/ppermute | solution.py:38
  23.5 7.4 %collective-permute-start.2 = (f32[5,2,1,258]{3,2,1,0:T(1,128)S(1)}, f32[5,2,1,258]{3,2,1,0:T(1,128)S(1)}, u32[]{:S(2)}, u32[]{:S(2)}) collective-permute-start(f32[5,2,1,258]{3,2,1,0:T(1,128)S(1)} %get-tuple-element.53), channel_id=1, source_target_pairs={{0,4},{4,8},{8,12},{12,16},{16,20},{20,24},{24,28},{28,32},{32,36}... | collective-permute-start | bytes 30968 | tf_op jit(solution)/shard_map/ppermute | solution.py:37
  28.6 8.0 %collective-permute-start.3 = (f32[5,2,1,258]{3,2,1,0:T(1,128)S(1)}, f32[5,2,1,258]{3,2,1,0:T(1,128)S(1)}, u32[]{:S(2)}, u32[]{:S(2)}) collective-permute-start(f32[5,2,1,258]{3,2,1,0:T(1,128)S(1)} %get-tuple-element.54), channel_id=1, source_target_pairs={{4,0},{8,4},{12,8},{16,12},{20,16},{24,20},{28,24},{32,28},{36,32}... | collective-permute-start | bytes 30968 | tf_op jit(solution)/shard_map/ppermute | solution.py:38
  37.7 13.0 %collective-permute-start.4 = (f32[5,1,66,258]{3,1,2,0:T(1,128)S(1)}, f32[5,1,66,258]{3,1,2,0:T(1,128)S(1)}, u32[]{:S(2)}, u32[]{:S(2)}) collective-permute-start(f32[5,1,66,258]{3,1,2,0:T(1,128)S(1)} %copy.8), channel_id=1, source_target_pairs={{0,1},{1,2},{2,3},{3,0},{4,5},{5,6},{6,7},{7,4},{8,9},{9,10},{10,1... | collective-permute-start | bytes 1021688 | tf_op jit(solution)/shard_map/ppermute | solution.py:37
  40.2 10.7 %collective-permute-start.5 = (f32[5,1,66,258]{3,1,2,0:T(1,128)S(1)}, f32[5,1,66,258]{3,1,2,0:T(1,128)S(1)}, u32[]{:S(2)}, u32[]{:S(2)}) collective-permute-start(f32[5,1,66,258]{3,1,2,0:T(1,128)S(1)} %copy.9), channel_id=1, source_target_pairs={{1,0},{2,1},{3,2},{0,3},{5,4},{6,5},{7,6},{4,7},{9,8},{10,9},{11,1... | collective-permute-start | bytes 1021688 | tf_op jit(solution)/shard_map/ppermute | solution.py:38
  53.6 171.5 %copy-start.1 = (s32[16]{0:T(128)S(1)}, s32[16]{0:T(128)}, u32[]{:S(2)}) copy-start(s32[16]{0:T(128)} %param.3) | copy-start | bytes 196
  221.7 5.6 %collective-permute-start.6 = (f32[1,1,10,256]{3,1,2,0:T(1,128)S(1)}, f32[1,1,10,256]{3,1,2,0:T(1,128)S(1)}, u32[]{:S(2)}, u32[]{:S(2)}) collective-permute-start(f32[1,1,10,256]{3,1,2,0:T(1,128)S(1)} %get-tuple-element.62), channel_id=1, source_target_pairs={{0,64},{64,0},{128,192},{192,128},{256,320},{320,256},{384,448},{4... | collective-permute-start | bytes 30728 | tf_op jit(solution)/shard_map/ppermute | solution.py:23
  227.3 6.6 %collective-permute-start.7 = (f32[2,1,10,256]{3,1,2,0:T(1,128)S(1)}, f32[2,1,10,256]{3,1,2,0:T(1,128)S(1)}, u32[]{:S(2)}, u32[]{:S(2)}) collective-permute-start(f32[2,1,10,256]{3,1,2,0:T(1,128)S(1)} %get-tuple-element.64), channel_id=1, source_target_pairs={{0,128},{64,192},{128,0},{192,64},{256,384},{320,448},{384,256},{4... | collective-permute-start | bytes 61448 | tf_op jit(solution)/shard_map/ppermute | solution.py:23
  234.0 10.6 %collective-permute-start.8 = (f32[4,1,10,256]{3,1,2,0:T(1,128)S(1)}, f32[4,1,10,256]{3,1,2,0:T(1,128)S(1)}, u32[]{:S(2)}, u32[]{:S(2)}) collective-permute-start(f32[4,1,10,256]{3,1,2,0:T(1,128)S(1)} %bitcast.68), channel_id=1, source_target_pairs={{0,256},{64,320},{128,384},{192,448},{256,0},{320,64},{384,128},{4... | collective-permute-start | bytes 122888 | tf_op jit(solution)/shard_map/ppermute | solution.py:23
Sparse Core Ops, SparseCore 0:
  55.5 165.2 all-reduce.1
